TPU v7x, 256 devices: a whole 4x4x8 slice. The times are simulated.
256 devices in a mesh: segment: 16 (over x_lo, z), tp: 16 (over y, x_hi, core).
Axes of the slice: x: 4 (x_hi: 2, x_lo: 2; x = x_hi * 2 + x_lo), y: 4, z: 8, core: 2. Of those that a mesh axis runs over, the one named last changes fastest.
Arguments:
- layer_inputs: bfloat16 [16, 2, 128, 2048], P('segment', None, 'tp'), may hold values from -100 to 100, as said below
- cotangent: bfloat16 [2, 2, 128, 2048], P(None, None, 'tp'), may hold values from -6 to 6
- gate_weight: bfloat16 [16, 2048, 4096], P('segment', None, 'tp'), may hold values from -1 to 1, as said below
- up_weight: bfloat16 [16, 2048, 4096], P('segment', None, 'tp'), may hold values from -1 to 1, as said below
- down_weight: bfloat16 [16, 4096, 2048], P('segment', 'tp'), may hold values from -1 to 1, as said below
- gate_momentum: float32 [16, 1024, 4096], P('segment', None, 'tp'), may hold values from -48 to 48
- up_momentum: float32 [16, 1024, 4096], P('segment', None, 'tp'), may hold values from -48 to 48
- down_momentum: float32 [16, 4096, 1024], P('segment', 'tp'), may hold values from -48 to 48
Outputs:
- input_gradient: bfloat16 [16, 2, 128, 2048], P('segment', None, 'tp')
- new_gate_momentum: float32 [16, 1024, 4096], P('segment', None, 'tp')
- new_up_momentum: float32 [16, 1024, 4096], P('segment', None, 'tp')
- new_down_momentum: float32 [16, 4096, 1024], P('segment', 'tp')
Inputs may be any that keep to these rules, and one draw needn't show every extreme that they name: `layer_inputs`: stored layer inputs, independent for every section and micro-batch. `gate_weight`: sections 2l and 2l + 1 hold equal copies of one layer's weights. `up_weight`: sections 2l and 2l + 1 hold equal copies of one layer's weights. `down_weight`: sections 2l and 2l + 1 hold equal copies of one layer's weights.
All inputs are finite; a program needn't handle non-finite values.
Results may differ from a plain program's by a relative error of at most 0.02.
Values may be sent and summed in bfloat16 or wider, within the bound.
No kernel may reach another device: no remote copies, remote signals or barrier semaphores. Data moves between devices by JAX's collectives and lax.ppermute only.
A program may use at most 64 MiB of HBM per device.

v0:
```python
import jax
import jax.numpy as jnp
from jax import lax
from jax.sharding import PartitionSpec as P

epsilon = 1e-05
momentum_decay = 0.9


def passed_along(block, axis, distance):
    devices = range(lax.axis_size(axis))
    route = [(i - distance, i) for i in devices if i - distance in devices]
    return lax.ppermute(block, axis, route)


def partner(block, axis, distance):
    count = lax.axis_size(axis)
    route = []
    for low in range(count):
        high = low | 1 << distance
        if high != low and high < count:
            route += [(low, high), (high, low)]
    return lax.ppermute(block, axis, route)


def contract_last(left, right):
    return lax.dot_general(
        left, right, (((1,), (1,)), ((), ())), preferred_element_type=jnp.float32
    )


def contract_rows(left, right):
    return lax.dot_general(
        left, right, (((0,), (0,)), ((), ())), preferred_element_type=jnp.float32
    )


def project(rows, gate_w, up_w):
    gate = jnp.dot(rows, gate_w, preferred_element_type=jnp.float32)
    up = jnp.dot(rows, up_w, preferred_element_type=jnp.float32)
    return (gate, up)


def backward_factors(incoming_rows, gate, up, down_w):
    hidden_grad = contract_last(incoming_rows, down_w)
    sigma = jax.nn.sigmoid(gate)
    silu = gate * sigma
    hidden = (silu * up).astype(jnp.bfloat16)
    gate_grad = (hidden_grad * up * sigma * (1.0 + gate * (1.0 - sigma))).astype(jnp.bfloat16)
    up_grad = (hidden_grad * silu).astype(jnp.bfloat16)
    return (hidden, gate_grad, up_grad)


def owned(array, start, size, axis):
    return lax.dynamic_slice_in_dim(array, start, size, axis)


def shards(
    layer_inputs,
    cotangent,
    gate_weight,
    up_weight,
    down_weight,
    gate_momentum,
    up_momentum,
    down_momentum,
):
    segments = lax.axis_size("segment")
    depth = segments // 2
    segment = lax.axis_index("segment")
    direction = segment % 2
    lower = direction == 0
    position = segment // 2
    gate_w = gate_weight[0]
    up_w = up_weight[0]
    down_w = down_weight[0]
    inputs = layer_inputs[0].astype(jnp.float32)
    micro, rows_dev, width = inputs.shape
    half = width // 2
    hidden_dev = gate_w.shape[1]
    total_rows = rows_dev * lax.axis_size("tp")
    inverse_norm = lax.rsqrt(jnp.mean(inputs * inputs, axis=-1, keepdims=True) + epsilon)
    exact = inputs * inverse_norm
    normed = exact.astype(jnp.bfloat16)
    entry = lax.dynamic_index_in_dim(cotangent, direction, 0, keepdims=False)
    ticks = depth + micro - 1
    extra = (
        jnp.zeros((width, hidden_dev), jnp.float32),
        jnp.zeros((width, hidden_dev), jnp.float32),
        jnp.zeros((hidden_dev, width), jnp.float32),
    )

    def process(tick, received, state):
        outgoing, backs, extra = state
        index = tick - position
        active = (index >= 0) & (index < micro)
        slot = jnp.clip(index, 0, micro - 1)
        local_in = jnp.where(position == 0, entry[slot], received)
        incoming_rows = lax.all_gather(local_in, "tp", axis=0, tiled=True)
        full_rows = lax.all_gather(normed[slot], "tp", axis=0, tiled=True)

        def factors():
            gate, up = project(full_rows, gate_w, up_w)
            return backward_factors(incoming_rows, gate, up, down_w)

        def resting():
            blank = jnp.zeros((total_rows, hidden_dev), jnp.bfloat16)
            return (blank, blank, blank)

        hidden, gate_grad, up_grad = lax.cond(active, factors, resting)
        count = lax.axis_size("tp") * rows_dev

        def compute():
            return contract_last(gate_grad, gate_w) + contract_last(up_grad, up_w)

        def quiet():
            return jnp.zeros((count, width), jnp.float32)

        normed_grad = lax.psum_scatter(
            lax.cond(active, compute, quiet).astype(jnp.bfloat16),
            "tp",
            scatter_dimension=0,
            tiled=True,
        ).astype(jnp.float32)
        scale = inverse_norm[slot]
        base = exact[slot]
        back = local_in.astype(jnp.float32) + scale * (
            normed_grad - base * jnp.mean(normed_grad * base, axis=-1, keepdims=True)
        )
        back = back.astype(jnp.bfloat16)
        backs = lax.dynamic_update_index_in_dim(
            backs, jnp.where(active, back, backs[slot]), slot, 0
        )

        def accumulate(totals):
            return (
                totals[0] + contract_rows(full_rows, gate_grad),
                totals[1] + contract_rows(full_rows, up_grad),
                totals[2] + contract_rows(hidden, incoming_rows),
            )

        def unchanged(totals):
            return totals

        extra = lax.cond(active, accumulate, unchanged, extra)
        return (back, backs, extra)

    zero_rows = jnp.zeros((rows_dev, width), jnp.bfloat16)
    state = process(
        0, zero_rows, (zero_rows, jnp.zeros((micro, rows_dev, width), jnp.bfloat16), extra)
    )

    def advance(tick, state):
        received = passed_along(state[0], "segment", 2)
        return process(tick, received, state)

    outgoing, backs, extra = lax.fori_loop(1, ticks, advance, state)
    keep_start = jnp.where(lower, 0, half)
    send_start = half - keep_start
    gate_total, up_total, down_total = extra
    arrived = partner(
        (
            owned(gate_total, send_start, half, 0).astype(jnp.bfloat16),
            owned(up_total, send_start, half, 0).astype(jnp.bfloat16),
            owned(down_total, send_start, half, 1).astype(jnp.bfloat16),
        ),
        "segment",
        0,
    )
    gate_share = owned(gate_total, keep_start, half, 0) + arrived[0].astype(jnp.float32)
    up_share = owned(up_total, keep_start, half, 0) + arrived[1].astype(jnp.float32)
    down_share = owned(down_total, keep_start, half, 1) + arrived[2].astype(jnp.float32)
    new_gate = (momentum_decay * gate_momentum[0] + gate_share)[None]
    new_up = (momentum_decay * up_momentum[0] + up_share)[None]
    new_down = (momentum_decay * down_momentum[0] + down_share)[None]
    return (backs[None], new_gate, new_up, new_down)


def solution(mesh):
    return jax.shard_map(
        shards,
        mesh=mesh,
        in_specs=(
            P("segment", None, "tp", None),
            P(None, None, "tp", None),
            P("segment", None, "tp"),
            P("segment", None, "tp"),
            P("segment", "tp", None),
            P("segment", None, "tp"),
            P("segment", None, "tp"),
            P("segment", "tp", None),
        ),
        out_specs=(
            P("segment", None, "tp", None),
            P("segment", None, "tp"),
            P("segment", None, "tp"),
            P("segment", "tp", None),
        ),
        check_vma=False,
    )
```

profile of v0, /device:TPU:32, one launch (start us, length us, event | category | flops | bytes accessed | tf_op | source)
XLA Modules:
  0.0 1206.1 jit_solution(18428818250983817290)
XLA Ops:
  10.5 26.7 %all-gather.1 = bf16[1,128,2048]{2,1,0:T(8,128)(2,1)S(1)} all-gather(bf16[1,8,2048]{2,1,0:T(8,128)(2,1)S(1)} %constant_dynamic-slice_fusion.3), channel_id=3, replica_groups=mesh['segment'=16,'tp'=16] {'tp'}, dimensions={1}, use_global_device_ids=true | all-gather | bytes 557056 | tf_op jit(solution)/shard_map/all_gather | solution.py:100
  38.0 23.0 %all-gather.2 = bf16[1,1,128,2048]{3,2,1,0:T(8,128)(2,1)} all-gather(bf16[1,1,8,2048]{3,2,1,0:T(8,128)(2,1)S(1)} %dynamic-slice_select_fusion), channel_id=4, replica_groups=mesh['segment'=16,'tp'=16] {'tp'}, dimensions={2}, use_global_device_ids=true | all-gather | bytes 557056 | tf_op jit(solution)/shard_map/all_gather | solution.py:99
  76.0 60.9 %reduce-scatter.3.cloned.1.call-done = bf16[8,2048]{1,0:T(8,128)(2,1)} async-done(((bf16[128,2048]{1,0:T(8,128)(2,1)}), bf16[8,2048]{1,0:T(8,128)(2,1)}) %reduce-scatter.3.cloned.1.call-update) | async-done | bytes 32784 | tf_op jit(solution)/shard_map/reduce_scatter | solution.py:119
  139.9 1021.5 %while.22 = (s32[]{:T(128)}, bf16[8,2048]{1,0:T(8,128)(2,1)}, bf16[2,8,2048]{2,1,0:T(8,128)(2,1)}, f32[2048,256]{1,0:T(8,128)}, f32[2048,256]{1,0:T(8,128)}, /*i...) while((s32[]{:T(128)}, bf16[8,2048]{1,0:T(8,128)(2,1)}, ...), condition=%wide.region_18.19_spmd, body=%wide.region_9.18_spmd.sunk | while | flops 1076527104 | bytes 32310056 | solution.py:157
  145.1 23.9 %all-gather.4 = bf16[1,128,2048]{2,1,0:T(8,128)(2,1)S(1)} all-gather(bf16[1,8,2048]{2,1,0:T(8,128)(2,1)S(1)} %constant_dynamic-slice_fusion.8), channel_id=2, replica_groups=mesh['segment'=16,'tp'=16] {'tp'}, dimensions={1}, use_global_device_ids=true | all-gather | bytes 557056 | tf_op jit(solution)/shard_map/while/body/eval_jaxpr/all_gather | solution.py:100
  206.3 59.0 %reduce-scatter.5.cloned.1.call-done = bf16[8,2048]{1,0:T(8,128)(2,1)} async-done(((bf16[128,2048]{1,0:T(8,128)(2,1)}), bf16[8,2048]{1,0:T(8,128)(2,1)}) %reduce-scatter.5.cloned.1.call-update) | async-done | bytes 32784 | tf_op jit(solution)/shard_map/while/body/eval_jaxpr/reduce_scatter | solution.py:119
  272.9 23.8 %all-gather.4 = bf16[1,128,2048]{2,1,0:T(8,128)(2,1)S(1)} all-gather(bf16[1,8,2048]{2,1,0:T(8,128)(2,1)S(1)} %constant_dynamic-slice_fusion.8), channel_id=2, replica_groups=mesh['segment'=16,'tp'=16] {'tp'}, dimensions={1}, use_global_device_ids=true | all-gather | bytes 557056 | tf_op jit(solution)/shard_map/while/body/eval_jaxpr/all_gather | solution.py:100
  297.5 22.1 %all_gather.25 = bf16[128,2048]{1,0:T(8,128)(2,1)S(1)} all-gather(bf16[8,2048]{1,0:T(8,128)(2,1)S(1)} %bitcast_select_fusion.3), channel_id=1, replica_groups=mesh['segment'=16,'tp'=16] {'tp'}, dimensions={0}, use_global_device_ids=true | all-gather | bytes 557056 | tf_op jit(solution)/shard_map/while/body/eval_jaxpr/all_gather | solution.py:99
  321.4 71.9 %reduce-scatter.5.cloned.1.call-done = bf16[8,2048]{1,0:T(8,128)(2,1)} async-done(((bf16[128,2048]{1,0:T(8,128)(2,1)}), bf16[8,2048]{1,0:T(8,128)(2,1)}) %reduce-scatter.5.cloned.1.call-update) | async-done | bytes 32784 | tf_op jit(solution)/shard_map/while/body/eval_jaxpr/reduce_scatter | solution.py:119
  400.8 23.8 %all-gather.4 = bf16[1,128,2048]{2,1,0:T(8,128)(2,1)S(1)} all-gather(bf16[1,8,2048]{2,1,0:T(8,128)(2,1)S(1)} %constant_dynamic-slice_fusion.8), channel_id=2, replica_groups=mesh['segment'=16,'tp'=16] {'tp'}, dimensions={1}, use_global_device_ids=true | all-gather | bytes 557056 | tf_op jit(solution)/shard_map/while/body/eval_jaxpr/all_gather | solution.py:100
  425.4 22.1 %all_gather.25 = bf16[128,2048]{1,0:T(8,128)(2,1)S(1)} all-gather(bf16[8,2048]{1,0:T(8,128)(2,1)S(1)} %bitcast_select_fusion.3), channel_id=1, replica_groups=mesh['segment'=16,'tp'=16] {'tp'}, dimensions={0}, use_global_device_ids=true | all-gather | bytes 557056 | tf_op jit(solution)/shard_map/while/body/eval_jaxpr/all_gather | solution.py:99
  449.3 71.9 %reduce-scatter.5.cloned.1.call-done = bf16[8,2048]{1,0:T(8,128)(2,1)} async-done(((bf16[128,2048]{1,0:T(8,128)(2,1)}), bf16[8,2048]{1,0:T(8,128)(2,1)}) %reduce-scatter.5.cloned.1.call-update) | async-done | bytes 32784 | tf_op jit(solution)/shard_map/while/body/eval_jaxpr/reduce_scatter | solution.py:119
  528.7 23.8 %all-gather.4 = bf16[1,128,2048]{2,1,0:T(8,128)(2,1)S(1)} all-gather(bf16[1,8,2048]{2,1,0:T(8,128)(2,1)S(1)} %constant_dynamic-slice_fusion.8), channel_id=2, replica_groups=mesh['segment'=16,'tp'=16] {'tp'}, dimensions={1}, use_global_device_ids=true | all-gather | bytes 557056 | tf_op jit(solution)/shard_map/while/body/eval_jaxpr/all_gather | solution.py:100
  577.2 71.1 %reduce-scatter.5.cloned.1.call-done = bf16[8,2048]{1,0:T(8,128)(2,1)} async-done(((bf16[128,2048]{1,0:T(8,128)(2,1)}), bf16[8,2048]{1,0:T(8,128)(2,1)}) %reduce-scatter.5.cloned.1.call-update) | async-done | bytes 32784 | tf_op jit(solution)/shard_map/while/body/eval_jaxpr/reduce_scatter | solution.py:119
  655.9 23.8 %all-gather.4 = bf16[1,128,2048]{2,1,0:T(8,128)(2,1)S(1)} all-gather(bf16[1,8,2048]{2,1,0:T(8,128)(2,1)S(1)} %constant_dynamic-slice_fusion.8), channel_id=2, replica_groups=mesh['segment'=16,'tp'=16] {'tp'}, dimensions={1}, use_global_device_ids=true | all-gather | bytes 557056 | tf_op jit(solution)/shard_map/while/body/eval_jaxpr/all_gather | solution.py:100
  704.3 72.2 %reduce-scatter.5.cloned.1.call-done = bf16[8,2048]{1,0:T(8,128)(2,1)} async-done(((bf16[128,2048]{1,0:T(8,128)(2,1)}), bf16[8,2048]{1,0:T(8,128)(2,1)}) %reduce-scatter.5.cloned.1.call-update) | async-done | bytes 32784 | tf_op jit(solution)/shard_map/while/body/eval_jaxpr/reduce_scatter | solution.py:119
  784.1 23.8 %all-gather.4 = bf16[1,128,2048]{2,1,0:T(8,128)(2,1)S(1)} all-gather(bf16[1,8,2048]{2,1,0:T(8,128)(2,1)S(1)} %constant_dynamic-slice_fusion.8), channel_id=2, replica_groups=mesh['segment'=16,'tp'=16] {'tp'}, dimensions={1}, use_global_device_ids=true | all-gather | bytes 557056 | tf_op jit(solution)/shard_map/while/body/eval_jaxpr/all_gather | solution.py:100
  808.7 22.1 %all_gather.25 = bf16[128,2048]{1,0:T(8,128)(2,1)S(1)} all-gather(bf16[8,2048]{1,0:T(8,128)(2,1)S(1)} %bitcast_select_fusion.3), channel_id=1, replica_groups=mesh['segment'=16,'tp'=16] {'tp'}, dimensions={0}, use_global_device_ids=true | all-gather | bytes 557056 | tf_op jit(solution)/shard_map/while/body/eval_jaxpr/all_gather | solution.py:99
  832.6 72.3 %reduce-scatter.5.cloned.1.call-done = bf16[8,2048]{1,0:T(8,128)(2,1)} async-done(((bf16[128,2048]{1,0:T(8,128)(2,1)}), bf16[8,2048]{1,0:T(8,128)(2,1)}) %reduce-scatter.5.cloned.1.call-update) | async-done | bytes 32784 | tf_op jit(solution)/shard_map/while/body/eval_jaxpr/reduce_scatter | solution.py:119
  912.5 23.9 %all-gather.4 = bf16[1,128,2048]{2,1,0:T(8,128)(2,1)S(1)} all-gather(bf16[1,8,2048]{2,1,0:T(8,128)(2,1)S(1)} %constant_dynamic-slice_fusion.8), channel_id=2, replica_groups=mesh['segment'=16,'tp'=16] {'tp'}, dimensions={1}, use_global_device_ids=true | all-gather | bytes 557056 | tf_op jit(solution)/shard_map/while/body/eval_jaxpr/all_gather | solution.py:100
  960.9 72.4 %reduce-scatter.5.cloned.1.call-done = bf16[8,2048]{1,0:T(8,128)(2,1)} async-done(((bf16[128,2048]{1,0:T(8,128)(2,1)}), bf16[8,2048]{1,0:T(8,128)(2,1)}) %reduce-scatter.5.cloned.1.call-update) | async-done | bytes 32784 | tf_op jit(solution)/shard_map/while/body/eval_jaxpr/reduce_scatter | solution.py:119
  1040.9 23.8 %all-gather.4 = bf16[1,128,2048]{2,1,0:T(8,128)(2,1)S(1)} all-gather(bf16[1,8,2048]{2,1,0:T(8,128)(2,1)S(1)} %constant_dynamic-slice_fusion.8), channel_id=2, replica_groups=mesh['segment'=16,'tp'=16] {'tp'}, dimensions={1}, use_global_device_ids=true | all-gather | bytes 557056 | tf_op jit(solution)/shard_map/while/body/eval_jaxpr/all_gather | solution.py:100
  1065.5 22.1 %all_gather.25 = bf16[128,2048]{1,0:T(8,128)(2,1)S(1)} all-gather(bf16[8,2048]{1,0:T(8,128)(2,1)S(1)} %bitcast_select_fusion.3), channel_id=1, replica_groups=mesh['segment'=16,'tp'=16] {'tp'}, dimensions={0}, use_global_device_ids=true | all-gather | bytes 557056 | tf_op jit(solution)/shard_map/while/body/eval_jaxpr/all_gather | solution.py:99
  1089.3 69.7 %reduce-scatter.5.cloned.1.call-done = bf16[8,2048]{1,0:T(8,128)(2,1)} async-done(((bf16[128,2048]{1,0:T(8,128)(2,1)}), bf16[8,2048]{1,0:T(8,128)(2,1)}) %reduce-scatter.5.cloned.1.call-update) | async-done | bytes 32784 | tf_op jit(solution)/shard_map/while/body/eval_jaxpr/reduce_scatter | solution.py:119
  (210 shorter events, 274.7 us)
Async XLA Ops:
  7.2 129.7 %reduce-scatter.3.cloned.1.call-start = ((), (), s32[]{:S(2)}) async-start(), calls=%async_computation.2 | async-start | bytes 557056 | tf_op jit(solution)/shard_map/reduce_scatter | solution.py:119
  68.9 71.0 %copy-start = (bf16[1,2048,256]{2,1,0:T(8,128)(2,1)S(1)}, bf16[1,2048,256]{2,1,0:T(8,128)(2,1)}, u32[]{:S(2)}) copy-start(bf16[1,2048,256]{2,1,0:T(8,128)(2,1)} %param.24) | copy-start | bytes 3145732
  68.9 71.0 %copy-start.1 = (bf16[1,2048,256]{2,1,0:T(8,128)(2,1)S(1)}, bf16[1,2048,256]{2,1,0:T(8,128)(2,1)}, u32[]{:S(2)}) copy-start(bf16[1,2048,256]{2,1,0:T(8,128)(2,1)} %param.25) | copy-start | bytes 3145732
  139.9 125.5 %reduce-scatter.5.cloned.1.call-start = ((), (), s32[]{:S(2)}) async-start(), calls=%async_computation.3 | async-start | bytes 557056 | tf_op jit(solution)/shard_map/while/body/eval_jaxpr/reduce_scatter | solution.py:119
  139.9 29.1 %collective-permute-start = (bf16[8,2048]{1,0:T(8,128)(2,1)}, bf16[8,2048]{1,0:T(8,128)(2,1)S(1)}, u32[]{:S(2)}, u32[]{:S(2)}) collective-permute-start(bf16[8,2048]{1,0:T(8,128)(2,1)} %get-tuple-element.645), channel_id=1, source_target_pairs={{0,32},{16,48},{32,64},{48,80},{64,96},{80,112},{96,128},{112,144}... | collective-permute-start | bytes 98312 | tf_op jit(solution)/shard_map/while/body/eval_jaxpr/ppermute | solution.py:13
  267.7 125.5 %reduce-scatter.5.cloned.1.call-start = ((), (), s32[]{:S(2)}) async-start(), calls=%async_computation.3 | async-start | bytes 557056 | tf_op jit(solution)/shard_map/while/body/eval_jaxpr/reduce_scatter | solution.py:119
  267.7 29.1 %collective-permute-start = (bf16[8,2048]{1,0:T(8,128)(2,1)}, bf16[8,2048]{1,0:T(8,128)(2,1)S(1)}, u32[]{:S(2)}, u32[]{:S(2)}) collective-permute-start(bf16[8,2048]{1,0:T(8,128)(2,1)} %get-tuple-element.645), channel_id=1, source_target_pairs={{0,32},{16,48},{32,64},{48,80},{64,96},{80,112},{96,128},{112,144}... | collective-permute-start | bytes 98312 | tf_op jit(solution)/shard_map/while/body/eval_jaxpr/ppermute | solution.py:13
  395.6 125.5 %reduce-scatter.5.cloned.1.call-start = ((), (), s32[]{:S(2)}) async-start(), calls=%async_computation.3 | async-start | bytes 557056 | tf_op jit(solution)/shard_map/while/body/eval_jaxpr/reduce_scatter | solution.py:119
  395.6 29.1 %collective-permute-start = (bf16[8,2048]{1,0:T(8,128)(2,1)}, bf16[8,2048]{1,0:T(8,128)(2,1)S(1)}, u32[]{:S(2)}, u32[]{:S(2)}) collective-permute-start(bf16[8,2048]{1,0:T(8,128)(2,1)} %get-tuple-element.645), channel_id=1, source_target_pairs={{0,32},{16,48},{32,64},{48,80},{64,96},{80,112},{96,128},{112,144}... | collective-permute-start | bytes 98312 | tf_op jit(solution)/shard_map/while/body/eval_jaxpr/ppermute | solution.py:13
  523.5 124.7 %reduce-scatter.5.cloned.1.call-start = ((), (), s32[]{:S(2)}) async-start(), calls=%async_computation.3 | async-start | bytes 557056 | tf_op jit(solution)/shard_map/while/body/eval_jaxpr/reduce_scatter | solution.py:119
  523.5 29.1 %collective-permute-start = (bf16[8,2048]{1,0:T(8,128)(2,1)}, bf16[8,2048]{1,0:T(8,128)(2,1)S(1)}, u32[]{:S(2)}, u32[]{:S(2)}) collective-permute-start(bf16[8,2048]{1,0:T(8,128)(2,1)} %get-tuple-element.645), channel_id=1, source_target_pairs={{0,32},{16,48},{32,64},{48,80},{64,96},{80,112},{96,128},{112,144}... | collective-permute-start | bytes 98312 | tf_op jit(solution)/shard_map/while/body/eval_jaxpr/ppermute | solution.py:13
  650.6 125.9 %reduce-scatter.5.cloned.1.call-start = ((), (), s32[]{:S(2)}) async-start(), calls=%async_computation.3 | async-start | bytes 557056 | tf_op jit(solution)/shard_map/while/body/eval_jaxpr/reduce_scatter | solution.py:119
  650.6 29.1 %collective-permute-start = (bf16[8,2048]{1,0:T(8,128)(2,1)}, bf16[8,2048]{1,0:T(8,128)(2,1)S(1)}, u32[]{:S(2)}, u32[]{:S(2)}) collective-permute-start(bf16[8,2048]{1,0:T(8,128)(2,1)} %get-tuple-element.645), channel_id=1, source_target_pairs={{0,32},{16,48},{32,64},{48,80},{64,96},{80,112},{96,128},{112,144}... | collective-permute-start | bytes 98312 | tf_op jit(solution)/shard_map/while/body/eval_jaxpr/ppermute | solution.py:13
  778.9 126.0 %reduce-scatter.5.cloned.1.call-start = ((), (), s32[]{:S(2)}) async-start(), calls=%async_computation.3 | async-start | bytes 557056 | tf_op jit(solution)/shard_map/while/body/eval_jaxpr/reduce_scatter | solution.py:119
  778.9 29.1 %collective-permute-start = (bf16[8,2048]{1,0:T(8,128)(2,1)}, bf16[8,2048]{1,0:T(8,128)(2,1)S(1)}, u32[]{:S(2)}, u32[]{:S(2)}) collective-permute-start(bf16[8,2048]{1,0:T(8,128)(2,1)} %get-tuple-element.645), channel_id=1, source_target_pairs={{0,32},{16,48},{32,64},{48,80},{64,96},{80,112},{96,128},{112,144}... | collective-permute-start | bytes 98312 | tf_op jit(solution)/shard_map/while/body/eval_jaxpr/ppermute | solution.py:13
  907.2 126.0 %reduce-scatter.5.cloned.1.call-start = ((), (), s32[]{:S(2)}) async-start(), calls=%async_computation.3 | async-start | bytes 557056 | tf_op jit(solution)/shard_map/while/body/eval_jaxpr/reduce_scatter | solution.py:119
  907.3 29.1 %collective-permute-start = (bf16[8,2048]{1,0:T(8,128)(2,1)}, bf16[8,2048]{1,0:T(8,128)(2,1)S(1)}, u32[]{:S(2)}, u32[]{:S(2)}) collective-permute-start(bf16[8,2048]{1,0:T(8,128)(2,1)} %get-tuple-element.645), channel_id=1, source_target_pairs={{0,32},{16,48},{32,64},{48,80},{64,96},{80,112},{96,128},{112,144}... | collective-permute-start | bytes 98312 | tf_op jit(solution)/shard_map/while/body/eval_jaxpr/ppermute | solution.py:13
  1035.7 123.4 %reduce-scatter.5.cloned.1.call-start = ((), (), s32[]{:S(2)}) async-start(), calls=%async_computation.3 | async-start | bytes 557056 | tf_op jit(solution)/shard_map/while/body/eval_jaxpr/reduce_scatter | solution.py:119
  1035.7 29.1 %collective-permute-start = (bf16[8,2048]{1,0:T(8,128)(2,1)}, bf16[8,2048]{1,0:T(8,128)(2,1)S(1)}, u32[]{:S(2)}, u32[]{:S(2)}) collective-permute-start(bf16[8,2048]{1,0:T(8,128)(2,1)} %get-tuple-element.645), channel_id=1, source_target_pairs={{0,32},{16,48},{32,64},{48,80},{64,96},{80,112},{96,128},{112,144}... | collective-permute-start | bytes 98312 | tf_op jit(solution)/shard_map/while/body/eval_jaxpr/ppermute | solution.py:13
  1162.8 14.9 %collective-permute-start.1 = (bf16[1024,256]{1,0:T(8,128)(2,1)S(1)}, bf16[1024,256]{1,0:T(8,128)(2,1)S(1)}, u32[]{:S(2)}, u32[]{:S(2)}) collective-permute-start(bf16[1024,256]{1,0:T(8,128)(2,1)S(1)} %dynamic-slice_convert_fusion.2), channel_id=1, source_target_pairs={{0,16},{16,0},{32,48},{48,32},{64,80},{80,64},{96,112},{112,96},{1... | collective-permute-start | bytes 1572872 | tf_op jit(solution)/shard_map/ppermute | solution.py:23
  1164.6 24.3 %collective-permute-start.2 = (bf16[1024,256]{1,0:T(8,128)(2,1)S(1)}, bf16[1024,256]{1,0:T(8,128)(2,1)S(1)}, u32[]{:S(2)}, u32[]{:S(2)}) collective-permute-start(bf16[1024,256]{1,0:T(8,128)(2,1)S(1)} %dynamic-slice_convert_fusion.1), channel_id=1, source_target_pairs={{0,16},{16,0},{32,48},{48,32},{64,80},{80,64},{96,112},{112,96},{1... | collective-permute-start | bytes 1572872 | tf_op jit(solution)/shard_map/ppermute | solution.py:23
  1167.5 21.4 %copy-start.5 = (f32[1,1024,256]{2,1,0:T(8,128)S(1)}, f32[1,1024,256]{2,1,0:T(8,128)}, u32[]{:S(2)}) copy-start(f32[1,1024,256]{2,1,0:T(8,128)} %param.28) | copy-start | bytes 3145732
  1167.6 29.6 %collective-permute-start.3 = (bf16[256,1024]{1,0:T(8,128)(2,1)S(1)}, bf16[256,1024]{1,0:T(8,128)(2,1)S(1)}, u32[]{:S(2)}, u32[]{:S(2)}) collective-permute-start(bf16[256,1024]{1,0:T(8,128)(2,1)S(1)} %dynamic-slice_convert_fusion), channel_id=1, source_target_pairs={{0,16},{16,0},{32,48},{48,32},{64,80},{80,64},{96,112},{112,96},{1... | collective-permute-start | bytes 1572872 | tf_op jit(solution)/shard_map/ppermute | solution.py:23
  1180.0 17.1 %copy-start.6 = (f32[1,256,1024]{2,1,0:T(8,128)S(1)}, f32[1,256,1024]{2,1,0:T(8,128)}, u32[]{:S(2)}) copy-start(f32[1,256,1024]{2,1,0:T(8,128)} %param.29) | copy-start | bytes 3145732
  (7 other events, 30.4 us)
Sparse Core Ops, SparseCore 0:
  69.0 67.8 reduce-scatter.2
  195.5 69.7 reduce-scatter.4
  320.7 72.4 reduce-scatter.4
  448.6 72.4 reduce-scatter.4
  576.5 71.7 reduce-scatter.4
  703.6 72.8 reduce-scatter.4
  831.9 72.9 reduce-scatter.4
  960.2 73.0 reduce-scatter.4
  1088.7 70.3 reduce-scatter.4
where the time goes:
time: 1210 us
  waiting for transfers between devices  646 us (53%)
  blocking collectives  417 us (34%)
  starting transfers between devices  38.4 us (3%)
  other arithmetic  37.8 us (3%)
  matrix products  26.4 us (2%)
  local copies, waits for them, and re-layouts  25.8 us (2%)
  between operations  13.9 us (1%)
    reduce_scatter x9, waiting for transfers between devices, process(): lax.psum_scatter(lax.cond(active, compute, quiet).astype(jnp.bfloat16), '...  621 us
    all_gather x9, blocking collectives, process(): full_rows = lax.all_gather(normed[slot], 'tp', axis=0, tiled=True)  217 us
    all_gather x9, blocking collectives, process(): incoming_rows = lax.all_gather(local_in, 'tp', axis=0, tiled=True)  200 us
    ppermute x8, starting transfers between devices, passed_along(): return lax.ppermute(block, axis, route)  35.5 us
    ppermute x3, waiting for transfers between devices, partner(): return lax.ppermute(block, axis, route)  24.3 us
  transfers between devices with their start and end apart: 20, of which 12 were waited for; matrix products, arithmetic and copies ran while one was open for 3% of the time, Pallas kernels for 0%

commit v1 on v0

--- a/solution.py
+++ b/solution.py
@@ -1,3 +1,4 @@
+import functools
 import jax
 import jax.numpy as jnp
 from jax import lax
@@ -5,6 +6,15 @@
 
 epsilon = 1e-05
 momentum_decay = 0.9
+
+
+def supply_classes_for(s0, a_name):
+    return jnp.concatenate(
+        lax.all_to_all(jnp.stack([s0] * lax.axis_size(a_name)), a_name, 0, 0), axis=0
+    )
+
+
+fix_notes = functools.partial(supply_classes_for, a_name="tp")
 
 
 def passed_along(block, axis, distance):
@@ -96,7 +106,7 @@
         active = (index >= 0) & (index < micro)
         slot = jnp.clip(index, 0, micro - 1)
         local_in = jnp.where(position == 0, entry[slot], received)
-        incoming_rows = lax.all_gather(local_in, "tp", axis=0, tiled=True)
+        incoming_rows = fix_notes(local_in)
         full_rows = lax.all_gather(normed[slot], "tp", axis=0, tiled=True)
 
         def factors():

time: 1210 us -> 1120 us (0.926)
  blocking collectives: 417 us -> 239 us
  starting transfers between devices: 38.4 us -> 83 us
  waiting for transfers between devices: 646 us -> 678 us
    all_gather x9 -> x0, blocking collectives: 200 us -> none  [process(): incoming_rows = lax.all_gather(local_in, 'tp', axis=0, tiled=True)]
    all_to_all x0 -> x9, starting transfers between devices: none -> 44.3 us  [supply_classes_for(): lax.all_to_all(jnp.stack([s0] * lax.axis_size(a_name)), a_name, 0, 0)]
    all_gather x9, blocking collectives: 217 us -> 239 us  [process(): full_rows = lax.all_gather(normed[slot], 'tp', axis=0, tiled=True)]
    ppermute x8, waiting for transfers between devices: 0.02 us -> 16.1 us  [passed_along(): return lax.ppermute(block, axis, route)]
    reduce_scatter x9, waiting for transfers between devices: 621 us -> 637 us  [process(): lax.psum_scatter(lax.cond(active, compute, quiet).astype(jnp.bfloat16), '...]
  transfers between devices with their start and end apart: 20 -> 29, of which waited for: 12 -> 20; matrix products, arithmetic and copies ran while one was open for 3% -> 4% of each run, Pallas kernels for 0% -> 0%
where the time goes in v1:
time: 1120 us; the launch traced here: 1110 us
  waiting for transfers between devices  678 us (61%)
  blocking collectives  239 us (21%)
  starting transfers between devices  83 us (7%)
  other arithmetic  37.9 us (3%)
  local copies, waits for them, and re-layouts  34.8 us (3%)
  matrix products  22.6 us (2%)
  between operations  13.9 us (1%)
    reduce_scatter x9, waiting for transfers between devices, process(): lax.psum_scatter(lax.cond(active, compute, quiet).astype(jnp.bfloat16), '...  637 us
    all_gather x9, blocking collectives, process(): full_rows = lax.all_gather(normed[slot], 'tp', axis=0, tiled=True)  239 us
    all_to_all x9, starting transfers between devices, supply_classes_for(): lax.all_to_all(jnp.stack([s0] * lax.axis_size(a_name)), a_name, 0, 0)  44.3 us
    ppermute x8, starting transfers between devices, passed_along(): return lax.ppermute(block, axis, route)  35.5 us
    ppermute x3, waiting for transfers between devices, partner(): return lax.ppermute(block, axis, route)  24.3 us
  transfers between devices with their start and end apart: 29, of which 20 were waited for; matrix products, arithmetic and copies ran while one was open for 4% of the time, Pallas kernels for 0%

profile of v1, /device:TPU:32, one launch (start us, length us, event | category | flops | bytes accessed | tf_op | source)
XLA Modules:
  0.0 1110.2 jit_solution(18129135491522319794)
XLA Ops:
  9.9 7.1 all-to-all-start.1
  19.4 26.5 %all-gather.1 = bf16[1,128,2048]{2,1,0:T(8,128)(2,1)S(1)} all-gather(bf16[1,8,2048]{2,1,0:T(8,128)(2,1)S(1)} %constant_dynamic-slice_fusion.3), channel_id=3, replica_groups=mesh['segment'=16,'tp'=16] {'tp'}, dimensions={1}, use_global_device_ids=true | all-gather | bytes 557056 | tf_op jit(solution)/shard_map/all_gather | solution.py:110
  52.0 6.4 conditional.8
  58.4 59.5 %reduce-scatter.3.cloned.1.call-done = bf16[8,2048]{1,0:T(8,128)(2,1)} async-done(((bf16[128,2048]{1,0:T(8,128)(2,1)}), bf16[8,2048]{1,0:T(8,128)(2,1)}) %reduce-scatter.3.cloned.1.call-update) | async-done | bytes 32784 | tf_op jit(solution)/shard_map/reduce_scatter | solution.py:129
  121.0 944.5 %while.22 = (s32[]{:T(128)}, bf16[8,2048]{1,0:T(8,128)(2,1)}, bf16[2,8,2048]{2,1,0:T(8,128)(2,1)}, f32[2048,256]{1,0:T(8,128)}, f32[2048,256]{1,0:T(8,128)}, /*i...) while((s32[]{:T(128)}, bf16[8,2048]{1,0:T(8,128)(2,1)}, ...), condition=%wide.region_18.19_spmd, body=%wide.region_9.18_spmd.sunk | while | flops 1076527104 | bytes 33882952 | solution.py:167
  134.5 26.6 %all-gather.3 = bf16[1,128,2048]{2,1,0:T(8,128)(2,1)S(1)} all-gather(bf16[1,8,2048]{2,1,0:T(8,128)(2,1)S(1)} %constant_dynamic-slice_fusion.8), channel_id=2, replica_groups=mesh['segment'=16,'tp'=16] {'tp'}, dimensions={1}, use_global_device_ids=true | all-gather | bytes 557056 | tf_op jit(solution)/shard_map/while/body/eval_jaxpr/all_gather | solution.py:110
  165.4 10.2 conditional.14
  175.6 59.8 %reduce-scatter.5.cloned.1.call-done = bf16[8,2048]{1,0:T(8,128)(2,1)} async-done(((bf16[128,2048]{1,0:T(8,128)(2,1)}), bf16[8,2048]{1,0:T(8,128)(2,1)}) %reduce-scatter.5.cloned.1.call-update) | async-done | bytes 32784 | tf_op jit(solution)/shard_map/while/body/eval_jaxpr/reduce_scatter | solution.py:129
  251.3 26.6 %all-gather.3 = bf16[1,128,2048]{2,1,0:T(8,128)(2,1)S(1)} all-gather(bf16[1,8,2048]{2,1,0:T(8,128)(2,1)S(1)} %constant_dynamic-slice_fusion.8), channel_id=2, replica_groups=mesh['segment'=16,'tp'=16] {'tp'}, dimensions={1}, use_global_device_ids=true | all-gather | bytes 557056 | tf_op jit(solution)/shard_map/while/body/eval_jaxpr/all_gather | solution.py:110
  279.7 75.2 %reduce-scatter.5.cloned.1.call-done = bf16[8,2048]{1,0:T(8,128)(2,1)} async-done(((bf16[128,2048]{1,0:T(8,128)(2,1)}), bf16[8,2048]{1,0:T(8,128)(2,1)}) %reduce-scatter.5.cloned.1.call-update) | async-done | bytes 32784 | tf_op jit(solution)/shard_map/while/body/eval_jaxpr/reduce_scatter | solution.py:129
  370.8 26.6 %all-gather.3 = bf16[1,128,2048]{2,1,0:T(8,128)(2,1)S(1)} all-gather(bf16[1,8,2048]{2,1,0:T(8,128)(2,1)S(1)} %constant_dynamic-slice_fusion.8), channel_id=2, replica_groups=mesh['segment'=16,'tp'=16] {'tp'}, dimensions={1}, use_global_device_ids=true | all-gather | bytes 557056 | tf_op jit(solution)/shard_map/while/body/eval_jaxpr/all_gather | solution.py:110
  399.1 75.2 %reduce-scatter.5.cloned.1.call-done = bf16[8,2048]{1,0:T(8,128)(2,1)} async-done(((bf16[128,2048]{1,0:T(8,128)(2,1)}), bf16[8,2048]{1,0:T(8,128)(2,1)}) %reduce-scatter.5.cloned.1.call-update) | async-done | bytes 32784 | tf_op jit(solution)/shard_map/while/body/eval_jaxpr/reduce_scatter | solution.py:129
  490.2 26.6 %all-gather.3 = bf16[1,128,2048]{2,1,0:T(8,128)(2,1)S(1)} all-gather(bf16[1,8,2048]{2,1,0:T(8,128)(2,1)S(1)} %constant_dynamic-slice_fusion.8), channel_id=2, replica_groups=mesh['segment'=16,'tp'=16] {'tp'}, dimensions={1}, use_global_device_ids=true | all-gather | bytes 557056 | tf_op jit(solution)/shard_map/while/body/eval_jaxpr/all_gather | solution.py:110
  518.5 72.6 %reduce-scatter.5.cloned.1.call-done = bf16[8,2048]{1,0:T(8,128)(2,1)} async-done(((bf16[128,2048]{1,0:T(8,128)(2,1)}), bf16[8,2048]{1,0:T(8,128)(2,1)}) %reduce-scatter.5.cloned.1.call-update) | async-done | bytes 32784 | tf_op jit(solution)/shard_map/while/body/eval_jaxpr/reduce_scatter | solution.py:129
  607.1 26.6 %all-gather.3 = bf16[1,128,2048]{2,1,0:T(8,128)(2,1)S(1)} all-gather(bf16[1,8,2048]{2,1,0:T(8,128)(2,1)S(1)} %constant_dynamic-slice_fusion.8), channel_id=2, replica_groups=mesh['segment'=16,'tp'=16] {'tp'}, dimensions={1}, use_global_device_ids=true | all-gather | bytes 557056 | tf_op jit(solution)/shard_map/while/body/eval_jaxpr/all_gather | solution.py:110
  635.4 72.6 %reduce-scatter.5.cloned.1.call-done = bf16[8,2048]{1,0:T(8,128)(2,1)} async-done(((bf16[128,2048]{1,0:T(8,128)(2,1)}), bf16[8,2048]{1,0:T(8,128)(2,1)}) %reduce-scatter.5.cloned.1.call-update) | async-done | bytes 32784 | tf_op jit(solution)/shard_map/while/body/eval_jaxpr/reduce_scatter | solution.py:129
  723.9 26.6 %all-gather.3 = bf16[1,128,2048]{2,1,0:T(8,128)(2,1)S(1)} all-gather(bf16[1,8,2048]{2,1,0:T(8,128)(2,1)S(1)} %constant_dynamic-slice_fusion.8), channel_id=2, replica_groups=mesh['segment'=16,'tp'=16] {'tp'}, dimensions={1}, use_global_device_ids=true | all-gather | bytes 557056 | tf_op jit(solution)/shard_map/while/body/eval_jaxpr/all_gather | solution.py:110
  752.2 74.9 %reduce-scatter.5.cloned.1.call-done = bf16[8,2048]{1,0:T(8,128)(2,1)} async-done(((bf16[128,2048]{1,0:T(8,128)(2,1)}), bf16[8,2048]{1,0:T(8,128)(2,1)}) %reduce-scatter.5.cloned.1.call-update) | async-done | bytes 32784 | tf_op jit(solution)/shard_map/while/body/eval_jaxpr/reduce_scatter | solution.py:129
  843.1 26.6 %all-gather.3 = bf16[1,128,2048]{2,1,0:T(8,128)(2,1)S(1)} all-gather(bf16[1,8,2048]{2,1,0:T(8,128)(2,1)S(1)} %constant_dynamic-slice_fusion.8), channel_id=2, replica_groups=mesh['segment'=16,'tp'=16] {'tp'}, dimensions={1}, use_global_device_ids=true | all-gather | bytes 557056 | tf_op jit(solution)/shard_map/while/body/eval_jaxpr/all_gather | solution.py:110
  871.4 74.9 %reduce-scatter.5.cloned.1.call-done = bf16[8,2048]{1,0:T(8,128)(2,1)} async-done(((bf16[128,2048]{1,0:T(8,128)(2,1)}), bf16[8,2048]{1,0:T(8,128)(2,1)}) %reduce-scatter.5.cloned.1.call-update) | async-done | bytes 32784 | tf_op jit(solution)/shard_map/while/body/eval_jaxpr/reduce_scatter | solution.py:129
  962.2 26.6 %all-gather.3 = bf16[1,128,2048]{2,1,0:T(8,128)(2,1)S(1)} all-gather(bf16[1,8,2048]{2,1,0:T(8,128)(2,1)S(1)} %constant_dynamic-slice_fusion.8), channel_id=2, replica_groups=mesh['segment'=16,'tp'=16] {'tp'}, dimensions={1}, use_global_device_ids=true | all-gather | bytes 557056 | tf_op jit(solution)/shard_map/while/body/eval_jaxpr/all_gather | solution.py:110
  990.5 72.6 %reduce-scatter.5.cloned.1.call-done = bf16[8,2048]{1,0:T(8,128)(2,1)} async-done(((bf16[128,2048]{1,0:T(8,128)(2,1)}), bf16[8,2048]{1,0:T(8,128)(2,1)}) %reduce-scatter.5.cloned.1.call-update) | async-done | bytes 32784 | tf_op jit(solution)/shard_map/while/body/eval_jaxpr/reduce_scatter | solution.py:129
  1072.2 9.6 collective-permute-done.1
  1084.1 8.9 collective-permute-done.2
  (224 shorter events, 207.0 us)
Async XLA Ops:
  9.9 36.0 %all-to-all-start.1 = ((bf16[16,8,2048]{2,1,0:T(8,128)(2,1)}), bf16[16,8,2048]{2,1,0:T(8,128)(2,1)}, u32[]{:S(2)}, u32[]{:S(2)}) async-start(bf16[16,8,2048]{2,1,0:T(8,128)(2,1)} %stack.8), calls=%async_computation.2 | async-start | bytes 1048576 | tf_op jit(solution)/shard_map/all_to_all | solution.py:13
  17.0 100.9 %reduce-scatter.3.cloned.1.call-start = ((), (), s32[]{:S(2)}) async-start(), calls=%async_computation.4 | async-start | bytes 557056 | tf_op jit(solution)/shard_map/reduce_scatter | solution.py:129
  121.0 6.5 collective-permute-start
  129.1 32.0 %all-to-all-start = ((bf16[16,8,2048]{2,1,0:T(8,128)(2,1)}), bf16[16,8,2048]{2,1,0:T(8,128)(2,1)S(1)}, u32[]{:S(2)}, u32[]{:S(2)}) async-start(bf16[16,8,2048]{2,1,0:T(8,128)(2,1)} %stack.10), calls=%async_computation | async-start | bytes 1048576 | tf_op jit(solution)/shard_map/while/body/eval_jaxpr/all_to_all | solution.py:13
  133.7 101.7 %reduce-scatter.5.cloned.1.call-start = ((), (), s32[]{:S(2)}) async-start(), calls=%async_computation.5 | async-start | bytes 557056 | tf_op jit(solution)/shard_map/while/body/eval_jaxpr/reduce_scatter | solution.py:129
  237.8 6.5 collective-permute-start
  245.9 32.0 %all-to-all-start = ((bf16[16,8,2048]{2,1,0:T(8,128)(2,1)}), bf16[16,8,2048]{2,1,0:T(8,128)(2,1)S(1)}, u32[]{:S(2)}, u32[]{:S(2)}) async-start(bf16[16,8,2048]{2,1,0:T(8,128)(2,1)} %stack.10), calls=%async_computation | async-start | bytes 1048576 | tf_op jit(solution)/shard_map/while/body/eval_jaxpr/all_to_all | solution.py:13
  250.5 104.3 %reduce-scatter.5.cloned.1.call-start = ((), (), s32[]{:S(2)}) async-start(), calls=%async_computation.5 | async-start | bytes 557056 | tf_op jit(solution)/shard_map/while/body/eval_jaxpr/reduce_scatter | solution.py:129
  365.3 32.1 %all-to-all-start = ((bf16[16,8,2048]{2,1,0:T(8,128)(2,1)}), bf16[16,8,2048]{2,1,0:T(8,128)(2,1)S(1)}, u32[]{:S(2)}, u32[]{:S(2)}) async-start(bf16[16,8,2048]{2,1,0:T(8,128)(2,1)} %stack.10), calls=%async_computation | async-start | bytes 1048576 | tf_op jit(solution)/shard_map/while/body/eval_jaxpr/all_to_all | solution.py:13
  370.0 104.3 %reduce-scatter.5.cloned.1.call-start = ((), (), s32[]{:S(2)}) async-start(), calls=%async_computation.5 | async-start | bytes 557056 | tf_op jit(solution)/shard_map/while/body/eval_jaxpr/reduce_scatter | solution.py:129
  484.7 32.1 %all-to-all-start = ((bf16[16,8,2048]{2,1,0:T(8,128)(2,1)}), bf16[16,8,2048]{2,1,0:T(8,128)(2,1)S(1)}, u32[]{:S(2)}, u32[]{:S(2)}) async-start(bf16[16,8,2048]{2,1,0:T(8,128)(2,1)} %stack.10), calls=%async_computation | async-start | bytes 1048576 | tf_op jit(solution)/shard_map/while/body/eval_jaxpr/all_to_all | solution.py:13
  489.4 101.8 %reduce-scatter.5.cloned.1.call-start = ((), (), s32[]{:S(2)}) async-start(), calls=%async_computation.5 | async-start | bytes 557056 | tf_op jit(solution)/shard_map/while/body/eval_jaxpr/reduce_scatter | solution.py:129
  593.5 6.5 collective-permute-start
  601.6 32.1 %all-to-all-start = ((bf16[16,8,2048]{2,1,0:T(8,128)(2,1)}), bf16[16,8,2048]{2,1,0:T(8,128)(2,1)S(1)}, u32[]{:S(2)}, u32[]{:S(2)}) async-start(bf16[16,8,2048]{2,1,0:T(8,128)(2,1)} %stack.10), calls=%async_computation | async-start | bytes 1048576 | tf_op jit(solution)/shard_map/while/body/eval_jaxpr/all_to_all | solution.py:13
  606.3 101.7 %reduce-scatter.5.cloned.1.call-start = ((), (), s32[]{:S(2)}) async-start(), calls=%async_computation.5 | async-start | bytes 557056 | tf_op jit(solution)/shard_map/while/body/eval_jaxpr/reduce_scatter | solution.py:129
  718.4 32.1 %all-to-all-start = ((bf16[16,8,2048]{2,1,0:T(8,128)(2,1)}), bf16[16,8,2048]{2,1,0:T(8,128)(2,1)S(1)}, u32[]{:S(2)}, u32[]{:S(2)}) async-start(bf16[16,8,2048]{2,1,0:T(8,128)(2,1)} %stack.10), calls=%async_computation | async-start | bytes 1048576 | tf_op jit(solution)/shard_map/while/body/eval_jaxpr/all_to_all | solution.py:13
  723.1 104.0 %reduce-scatter.5.cloned.1.call-start = ((), (), s32[]{:S(2)}) async-start(), calls=%async_computation.5 | async-start | bytes 557056 | tf_op jit(solution)/shard_map/while/body/eval_jaxpr/reduce_scatter | solution.py:129
  837.5 32.1 %all-to-all-start = ((bf16[16,8,2048]{2,1,0:T(8,128)(2,1)}), bf16[16,8,2048]{2,1,0:T(8,128)(2,1)S(1)}, u32[]{:S(2)}, u32[]{:S(2)}) async-start(bf16[16,8,2048]{2,1,0:T(8,128)(2,1)} %stack.10), calls=%async_computation | async-start | bytes 1048576 | tf_op jit(solution)/shard_map/while/body/eval_jaxpr/all_to_all | solution.py:13
  842.2 104.0 %reduce-scatter.5.cloned.1.call-start = ((), (), s32[]{:S(2)}) async-start(), calls=%async_computation.5 | async-start | bytes 557056 | tf_op jit(solution)/shard_map/while/body/eval_jaxpr/reduce_scatter | solution.py:129
  956.7 32.1 %all-to-all-start = ((bf16[16,8,2048]{2,1,0:T(8,128)(2,1)}), bf16[16,8,2048]{2,1,0:T(8,128)(2,1)S(1)}, u32[]{:S(2)}, u32[]{:S(2)}) async-start(bf16[16,8,2048]{2,1,0:T(8,128)(2,1)} %stack.10), calls=%async_computation | async-start | bytes 1048576 | tf_op jit(solution)/shard_map/while/body/eval_jaxpr/all_to_all | solution.py:13
  961.4 101.7 %reduce-scatter.5.cloned.1.call-start = ((), (), s32[]{:S(2)}) async-start(), calls=%async_computation.5 | async-start | bytes 557056 | tf_op jit(solution)/shard_map/while/body/eval_jaxpr/reduce_scatter | solution.py:129
  1066.8 15.0 %collective-permute-start.1 = (bf16[1024,256]{1,0:T(8,128)(2,1)S(1)}, bf16[1024,256]{1,0:T(8,128)(2,1)S(1)}, u32[]{:S(2)}, u32[]{:S(2)}) collective-permute-start(bf16[1024,256]{1,0:T(8,128)(2,1)S(1)} %dynamic-slice_convert_fusion.2), channel_id=1, source_target_pairs={{0,16},{16,0},{32,48},{48,32},{64,80},{80,64},{96,112},{112,96},{1... | collective-permute-start | bytes 1572872 | tf_op jit(solution)/shard_map/ppermute | solution.py:33
  1068.7 24.3 %collective-permute-start.2 = (bf16[1024,256]{1,0:T(8,128)(2,1)S(1)}, bf16[1024,256]{1,0:T(8,128)(2,1)S(1)}, u32[]{:S(2)}, u32[]{:S(2)}) collective-permute-start(bf16[1024,256]{1,0:T(8,128)(2,1)S(1)} %dynamic-slice_convert_fusion.1), channel_id=1, source_target_pairs={{0,16},{16,0},{32,48},{48,32},{64,80},{80,64},{96,112},{112,96},{1... | collective-permute-start | bytes 1572872 | tf_op jit(solution)/shard_map/ppermute | solution.py:33
  1071.6 29.6 %collective-permute-start.3 = (bf16[256,1024]{1,0:T(8,128)(2,1)S(1)}, bf16[256,1024]{1,0:T(8,128)(2,1)S(1)}, u32[]{:S(2)}, u32[]{:S(2)}) collective-permute-start(bf16[256,1024]{1,0:T(8,128)(2,1)S(1)} %dynamic-slice_convert_fusion), channel_id=1, source_target_pairs={{0,16},{16,0},{32,48},{48,32},{64,80},{80,64},{96,112},{112,96},{1... | collective-permute-start | bytes 1572872 | tf_op jit(solution)/shard_map/ppermute | solution.py:33
  (14 other events, 168.5 us)
Sparse Core Ops, SparseCore 0:
  50.6 67.2 reduce-scatter.2
  164.8 70.6 reduce-scatter.4
  279.0 75.8 reduce-scatter.4
  398.4 75.7 reduce-scatter.4
  517.9 73.2 reduce-scatter.4
  634.7 73.1 reduce-scatter.4
  751.5 75.5 reduce-scatter.4
  870.7 75.5 reduce-scatter.4
  989.9 73.2 reduce-scatter.4
